TPU v7x, 32 devices: a whole 2x2x4 slice. The times are simulated.
32 devices in a mesh: group: 2 (over x), feat: 16 (over z, y, core).
Axes of the slice: x: 2, y: 2, z: 4, core: 2. Of those that a mesh axis runs over, the one named last changes fastest.
Arguments:
- hidden: bfloat16 [8192, 14336], P('group', 'feat'), parts along dimension 0, may hold values from -8 to 8
- grad_out: bfloat16 [8192, 4096], P('group', 'feat'), parts along dimension 0, may hold values from -8 to 8
- proj_in: bfloat16 [14336, 128], P('feat'), may hold values from -0.046875 to 0.046875
- proj_out: bfloat16 [4096, 128], P('feat'), may hold values from -0.09375 to 0.09375
- inv_out: float32 [128, 128], replicated, may hold values from -0.5 to 0.5
- inv_in: float32 [128, 128], replicated, may hold values from -0.5 to 0.5
- queries: bfloat16 [8192, 16384], P(None, 'feat'), may hold values from -0.01171875 to 0.01171875
Outputs:
- scores: float32 [8192, 256], P('feat', 'group'), parts along dimension 1
There are 2 independent parts, one for each index of `group`. A program takes and returns all parts, laid end to end along the dimension named above; an argument that names none is the same for every part. Nothing has to cross between parts.
All inputs are finite; a program needn't handle non-finite values.
Results may differ from a plain program's by a relative error of at most 0.005.
Values may be sent and summed in bfloat16 or wider, within the bound.
A program may use at most 64 MiB of HBM per device.

v0:
```python
import jax
import jax.numpy as jnp
from jax import lax
from jax.sharding import PartitionSpec as P

L = 32


def on_device(hidden, grad_out, proj_in, proj_out, inv_out, inv_in, queries):
    count_dev = lax.axis_size("feat")
    tok_rows = hidden.shape[0] // count_dev
    rank = proj_in.shape[1]
    in_part = jnp.dot(hidden, proj_in, preferred_element_type=jnp.float32)
    out_part = jnp.dot(grad_out, proj_out, preferred_element_type=jnp.float32)
    low_rows = lax.psum_scatter(
        jnp.concatenate([in_part, out_part], axis=1), "feat", scatter_dimension=0, tiled=True
    )
    in_low = low_rows[:, :rank].astype(jnp.bfloat16)
    out_low = low_rows[:, rank:].astype(jnp.bfloat16)
    seq_count = tok_rows // L
    in_seq = in_low.reshape(seq_count, L, rank)
    out_seq = out_low.reshape(seq_count, L, rank)
    per_example = jnp.einsum("elo,eli->eoi", out_seq, in_seq, preferred_element_type=jnp.float32)
    left = jnp.einsum("po,eoi->epi", inv_out, per_example, precision=lax.Precision.HIGHEST)
    conditioned = jnp.einsum("epi,iq->epq", left, inv_in, precision=lax.Precision.HIGHEST)
    conditioned = conditioned.reshape(seq_count, rank * rank).astype(jnp.bfloat16)
    contract = (((1,), (1,)), ((), ()))
    tiles = lax.all_to_all(conditioned, "feat", split_axis=1, concat_axis=0, tiled=True)
    return lax.psum_scatter(
        lax.dot_general(queries, tiles, contract, preferred_element_type=jnp.float32),
        "feat",
        scatter_dimension=0,
        tiled=True,
    )


def solution(mesh):
    placed = (
        P("group", "feat"),
        P("group", "feat"),
        P("feat", None),
        P("feat", None),
        P(),
        P(),
        P(None, "feat"),
    )
    return jax.shard_map(
        on_device, mesh=mesh, in_specs=placed, out_specs=P("feat", "group"), check_vma=False
    )
```

profile of v0, /device:TPU:0, one launch (start us, length us, event | category | flops | bytes accessed | tf_op | source)
XLA Modules:
  0.0 200.7 jit_solution(7296322471057407214)
XLA Ops:
  6.5 0.0 copy-start
  6.5 0.0 copy-start.1
  6.5 0.0 reduce-scatter.3.cloned.1.call-start
  6.5 5.7 %fusion.4 = f32[4096,128]{0,1:T(8,128)S(1)} fusion(bf16[4096,896]{1,0:T(8,128)(2,1)} %param.7, bf16[896,128]{1,0:T(8,128)(2,1)} %param.9), kind=kOutput, calls=%fused_computation.8 | convolution fusion | flops 939524096 | bytes 9666560 | tf_op jit(solution)/shard_map/dot_general | solution.py:13
  12.2 0.0 copy-done
  12.3 0.0 copy-done.1
  12.3 0.8 fusion.5
  13.1 2.4 %pad_maximum_fusion = f32[4096,256]{0,1:T(8,128)} fusion(f32[4096,128]{0,1:T(8,128)S(1)} %fusion.5, f32[4096,128]{0,1:T(8,128)S(1)} %fusion.4), kind=kLoop, calls=%fused_computation.1 | loop fusion | flops 1048576 | bytes 8388608 | tf_op jit(solution)/shard_map/concatenate | solution.py:16
  15.4 0.0 copy-start.2
  15.4 0.0 copy-start.3
  15.4 0.0 reduce-scatter.3.cloned.1.call-update
  15.5 0.0 reduce-scatter.5.cloned.1.call-start
  15.5 75.5 %reduce-scatter.3.cloned.1.call-done = f32[256,256]{0,1:T(8,128)} async-done(((f32[4096,256]{0,1:T(8,128)}), f32[256,256]{0,1:T(8,128)}) %reduce-scatter.3.cloned.1.call-update) | async-done | bytes 262160 | tf_op jit(solution)/shard_map/reduce_scatter | solution.py:15
  91.1 1.0 convert.4
  92.1 0.1 copy.10
  92.2 0.1 copy.9
  92.3 0.3 fusion.6
  92.6 0.0 copy-done.2
  92.6 0.6 convolution_bitcast_fusion.1
  93.2 0.0 copy-done.3
  93.2 0.6 convolution_convert_fusion
  93.8 0.1 convert_element_type.10
  93.9 0.2 copy.11
  94.1 13.6 %all_to_all.16 = bf16[8,16,1024]{2,0,1:T(8,128)(2,1)S(1)} all-to-all(bf16[8,16,1024]{2,0,1:T(8,128)(2,1)S(1)} %copy.11), channel_id=1, replica_groups=mesh['group'=2,'feat'=16] {'feat'}, dimensions={1} | all-to-all | bytes 524288 | tf_op jit(solution)/shard_map/all_to_all | solution.py:28
  107.6 13.2 %convolution_bitcast_fusion = f32[8192,128]{0,1:T(8,128)} fusion(bf16[8192,1024]{1,0:T(8,128)(2,1)} %param.13, bf16[8,16,1024]{2,0,1:T(8,128)(2,1)S(1)} %all_to_all.16), kind=kOutput, calls=%fused_computation | convolution fusion | flops 2147483648 | bytes 21233664 | tf_op jit(solution)/shard_map/dot_general | solution.py:30
  120.9 0.0 reduce-scatter.5.cloned.1.call-update
  120.9 71.2 %reduce-scatter.5.cloned.1.call-done = f32[512,128]{0,1:T(8,128)} async-done(((f32[8192,128]{0,1:T(8,128)}), f32[512,128]{0,1:T(8,128)}) %reduce-scatter.5.cloned.1.call-update) | async-done | bytes 262160 | tf_op jit(solution)/shard_map/reduce_scatter | solution.py:29
  192.1 1.8 copy.12
  (1 shorter events, 0.0 us)
Async XLA Ops:
  6.5 5.7 %copy-start = (bf16[4096,256]{1,0:T(8,128)(2,1)S(1)}, bf16[4096,256]{1,0:T(8,128)(2,1)}, u32[]{:S(2)}) copy-start(bf16[4096,256]{1,0:T(8,128)(2,1)} %param.8) | copy-start | bytes 6291460
  6.5 5.7 %copy-start.1 = (bf16[256,128]{1,0:T(8,128)(2,1)S(1)}, bf16[256,128]{1,0:T(8,128)(2,1)}, u32[]{:S(2)}) copy-start(bf16[256,128]{1,0:T(8,128)(2,1)} %param.10) | copy-start | bytes 196612
  6.5 84.5 %reduce-scatter.3.cloned.1.call-start = ((), (), s32[]{:S(2)}) async-start(), calls=%async_computation.3 | async-start | bytes 4456448 | tf_op jit(solution)/shard_map/reduce_scatter | solution.py:15
  15.4 77.1 %copy-start.2 = (f32[128,128]{1,0:T(8,128)S(1)}, f32[128,128]{1,0:T(8,128)}, u32[]{:S(2)}) copy-start(f32[128,128]{1,0:T(8,128)} %param.11) | copy-start | bytes 196612
  15.4 77.8 %copy-start.3 = (f32[128,128]{1,0:T(8,128)S(1)}, f32[128,128]{1,0:T(8,128)}, u32[]{:S(2)}) copy-start(f32[128,128]{1,0:T(8,128)} %param.12) | copy-start | bytes 196612
  15.5 176.6 %reduce-scatter.5.cloned.1.call-start = ((), (), s32[]{:S(2)}) async-start(), calls=%async_computation.4 | async-start | bytes 4456448 | tf_op jit(solution)/shard_map/reduce_scatter | solution.py:29
Sparse Core Ops, SparseCore 0:
  15.6 75.4 reduce-scatter.2
  121.0 71.0 reduce-scatter.4
where the time goes:
time: 201 us
  waiting for transfers between devices  147 us (73%)
  matrix products  21.2 us (11%)
  blocking collectives  13.6 us (7%)
  between operations  13.5 us (7%)
  other arithmetic  3.32 us (2%)
  local copies, waits for them, and re-layouts  2.3 us (1%)
    reduce_scatter x1, waiting for transfers between devices, on_device(): lax.psum_scatter(jnp.concatenate([in_part, out_part], axis=1), 'feat', sc...  75.5 us
    reduce_scatter x1, waiting for transfers between devices, on_device(): lax.psum_scatter(lax.dot_general(queries, tiles, contract, preferred_elem...  71.2 us
    all_to_all x1, blocking collectives, on_device(): lax.all_to_all(conditioned, 'feat', split_axis=1, concat_axis=0, tiled=True)  13.6 us
    dot_general x1, matrix products, on_device(): lax.dot_general(queries, tiles, contract, preferred_element_type=jnp.floa...  13.2 us
    dot_general x1, matrix products, on_device(): in_part = jnp.dot(hidden, proj_in, preferred_element_type=jnp.float32)  5.7 us
  transfers between devices with their start and end apart: 2, of which 2 were waited for; matrix products, arithmetic and copies ran while one was open for 0% of the time, Pallas kernels for 0%

commit v1 on v0

v1 whole, which is shorter than its diff:
```python
import functools

import jax
import jax.numpy as jnp
from jax import lax
from jax.experimental import pallas as pl
from jax.experimental.pallas import tpu as pltpu
from jax.sharding import PartitionSpec as P

L = 32
LANES = 128
SCALE = 2.0 ** 48
F32 = jnp.float32
BF16 = jnp.bfloat16
EXACT = lax.Precision.HIGHEST


def plain(hidden, grad_out, proj_in, proj_out, inv_out, inv_in, queries):
    count_dev = lax.axis_size("feat")
    tok_rows = hidden.shape[0] // count_dev
    rank = proj_in.shape[1]
    in_part = jnp.dot(hidden, proj_in, preferred_element_type=F32)
    out_part = jnp.dot(grad_out, proj_out, preferred_element_type=F32)
    low_rows = lax.psum_scatter(
        jnp.concatenate([in_part, out_part], axis=1), "feat", scatter_dimension=0, tiled=True
    )
    in_low = low_rows[:, :rank].astype(BF16)
    out_low = low_rows[:, rank:].astype(BF16)
    seq_count = tok_rows // L
    in_seq = in_low.reshape(seq_count, L, rank)
    out_seq = out_low.reshape(seq_count, L, rank)
    per_example = jnp.einsum("elo,eli->eoi", out_seq, in_seq, preferred_element_type=F32)
    left = jnp.einsum("po,eoi->epi", inv_out, per_example, precision=EXACT)
    conditioned = jnp.einsum("epi,iq->epq", left, inv_in, precision=EXACT)
    conditioned = conditioned.reshape(seq_count, rank * rank).astype(BF16)
    contract = (((1,), (1,)), ((), ()))
    tiles = lax.all_to_all(conditioned, "feat", split_axis=1, concat_axis=0, tiled=True)
    return lax.psum_scatter(
        lax.dot_general(queries, tiles, contract, preferred_element_type=F32),
        "feat",
        scatter_dimension=0,
        tiled=True,
    )


def code_square(x):
    x = x * SCALE
    return (x * jnp.abs(x)).astype(BF16)


def decode_square(y):
    y = y.astype(F32)
    root = jnp.sqrt(jnp.abs(y)) * (1.0 / SCALE)
    return jnp.where(y < 0, -root, root)


def code_plain(x):
    return x.astype(BF16)


def decode_plain(y):
    return y.astype(F32)


class Scatter:
    def __init__(self, n, me, rows, bufs, sems, code, decode, product):
        self.steps = n // 4
        self.c, self.b, self.a = me % 2, (me // 2) % 2, me // 4
        self.me, self.rows = me, rows
        self.own, self.csend, self.crecv, self.ysend, self.yrecv, self.zsend, self.zrecv = bufs
        self.sems = sems
        self.code, self.decode, self.product = code, decode, product

    def target(self, t):
        return (self.a + 1 + t) % self.steps

    def copy(self, stage, t, src, dst, to):
        return pltpu.make_async_remote_copy(
            src_ref=src.at[t], dst_ref=dst.at[t],
            send_sem=self.sems.at[stage, 0, t], recv_sem=self.sems.at[stage, 1, t],
            device_id={"feat": to}, device_id_type=pl.DeviceIdType.MESH,
        )

    def core(self, t):
        return self.copy(0, t, self.csend, self.crecv, self.me + 1 - 2 * self.c)

    def side(self, t):
        return self.copy(1, t, self.ysend, self.yrecv, self.me + 2 - 4 * self.b)

    def far(self, t):
        return self.copy(2, t, self.zsend, self.zrecv, self.target(t) * 4 + self.me % 4)

    def compute_send(self, t):
        for b in range(2):
            self.csend[t, b] = self.product((self.target(t) * 2 + b) * 2 + 1 - self.c).astype(self.csend.dtype)

    def compute_own(self, t):
        for b in range(2):
            self.own[t, b] = self.product((self.target(t) * 2 + b) * 2 + self.c)

    def stage_y(self, t):
        self.core(t).wait_recv()
        other = 1 - self.b
        self.ysend[t] = self.code(self.own[t, other] + self.crecv[t, other].astype(F32))
        self.side(t).start()

    def held(self, t):
        self.side(t).wait_recv()
        return self.own[t, self.b] + self.crecv[t, self.b].astype(F32) + self.decode(self.yrecv[t])

    def stage_z(self, t):
        self.zsend[t] = self.code(self.held(t))
        self.far(t).start()

    def run(self, ready, entered):
        last = self.steps - 1
        for i in range(self.steps + 2):
            if i < self.steps:
                ready(i)
                self.compute_send(i)
                if i == 0:
                    entered()
                self.core(i).start()
                self.compute_own(i)
            if 0 <= i - 1 < self.steps:
                self.stage_y(i - 1)
            if 0 <= i - 3 < last:
                self.stage_z(i - 3)
        for t in range(max(self.steps - 1, 0), last):
            self.stage_z(t)
        total = self.held(last)
        for t in range(last):
            self.far(t).wait_recv()
            total = total + self.decode(self.zrecv[t])
        return total

    def finish(self):
        for t in range(self.steps):
            self.core(t).wait_send()
            self.side(t).wait_send()
            if t < self.steps - 1:
                self.far(t).wait_send()


def kernel(n, hid_hbm, grad_hbm, pin_ref, pout_ref, iout_ref, iin_ref, que_hbm, out_ref,
           hid, grad, que, low_in, low_out, condf, cond, got, ct,
           own1, cs1, cr1, ys1, yr1, zs1, zr1,
           own2, cs2, cr2, ys2, yr2, zs2, zr2,
           load_sems, sems1, sems2, a2a_sems):
    me = lax.axis_index("feat")
    steps = n // 4
    rank = pin_ref.shape[1]
    tok = hid.shape[0] // n
    seqs = tok // L
    qrows = que.shape[0] // n
    local_p = rank // n

    barrier = pltpu.get_barrier_semaphore()
    for j in range(1, n):
        pl.semaphore_signal(barrier, inc=1, device_id={"feat": (me + j) % n},
                            device_id_type=pl.DeviceIdType.MESH)

    def entered():
        pl.semaphore_wait(barrier, n - 1)

    def project(chunk):
        at = pl.ds(pl.multiple_of(chunk * tok, tok), tok)
        return jnp.concatenate([
            jnp.dot(hid[at, :], pin_ref[...], preferred_element_type=F32),
            jnp.dot(grad[at, :], pout_ref[...], preferred_element_type=F32),
        ], axis=1)

    def score(chunk):
        at = pl.ds(pl.multiple_of(chunk * qrows, qrows), qrows)
        return lax.dot_general(que[at, :], ct[...], (((1,), (1,)), ((), ())), preferred_element_type=F32)

    first = Scatter(n, me, tok, (own1, cs1, cr1, ys1, yr1, zs1, zr1), sems1, code_square, decode_square, project)
    second = Scatter(n, me, qrows, (own2, cs2, cr2, ys2, yr2, zs2, zr2), sems2, code_plain, decode_plain, score)

    def load(hbm, vmem, which, t):
        size = hbm.shape[0] // steps
        at = pl.ds(pl.multiple_of(first.target(t) * size, size), size)
        return pltpu.make_async_copy(hbm.at[at, :], vmem.at[at, :], load_sems.at[which, t])

    for t in range(steps):
        load(hid_hbm, hid, 0, t).start()
        load(grad_hbm, grad, 1, t).start()

    def ready1(t):
        load(hid_hbm, hid, 0, t).wait()
        load(grad_hbm, grad, 1, t).wait()
        if t == steps - 1:
            for s in range(steps):
                load(que_hbm, que, 2, s).start()

    low = first.run(ready1, entered)

    low_in[...] = jnp.dot(low[:, :rank], iin_ref[...], precision=EXACT, preferred_element_type=F32)
    low_out[...] = lax.dot_general(low[:, rank:], iout_ref[...], (((1,), (1,)), ((), ())),
                                   precision=EXACT, preferred_element_type=F32)
    for e in range(seqs):
        at = pl.ds(e * L, L)
        condf[:, e, :] = lax.dot_general(low_out[at, :], low_in[at, :], (((0,), (0,)), ((), ())),
                                         precision=EXACT, preferred_element_type=F32)
    cond[...] = condf[...].reshape(n, local_p * seqs, rank).astype(BF16)

    def tile(j, slot):
        return pltpu.make_async_remote_copy(
            src_ref=cond.at[(me + j) % n], dst_ref=got.at[slot],
            send_sem=a2a_sems.at[0, j], recv_sem=a2a_sems.at[1, j],
            device_id={"feat": (me + j) % n}, device_id_type=pl.DeviceIdType.MESH,
        )

    for j in range(1, n):
        tile(j, me).start()
    got[me] = cond[me]
    for j in range(1, n):
        tile(j, (me + n - j) % n).wait_recv()
    for p in range(local_p):
        parts = got[...].astype(F32).reshape(n, local_p, seqs, rank)[:, p]
        ct[:, p * rank:(p + 1) * rank] = parts.reshape(n * seqs, rank).astype(BF16)

    def ready2(t):
        load(que_hbm, que, 2, t).wait()

    out_ref[...] = second.run(ready2, lambda: None)
    first.finish()
    second.finish()
    for j in range(1, n):
        tile(j, me).wait_send()


def scatter_scratch(steps, rows, cols, core_type):
    far = max(steps - 1, 1)
    return [
        pltpu.VMEM((steps, 2, rows, cols), F32),
        pltpu.VMEM((steps, 2, rows, cols), core_type),
        pltpu.VMEM((steps, 2, rows, cols), core_type),
        pltpu.VMEM((steps, rows, cols), BF16),
        pltpu.VMEM((steps, rows, cols), BF16),
        pltpu.VMEM((far, rows, cols), BF16),
        pltpu.VMEM((far, rows, cols), BF16),
    ]


def on_device(hidden, grad_out, proj_in, proj_out, inv_out, inv_in, queries):
    n = lax.axis_size("feat")
    tokens, rank = hidden.shape[0], proj_in.shape[1]
    tok = tokens // n
    seqs = tok // L
    fits = (
        n % 4 == 0 and n > 4 and rank == LANES and rank % n == 0 and tok % L == 0 and seqs % 8 == 0
        and hidden.shape[1] % LANES == 0 and grad_out.shape[1] % LANES == 0
        and queries.shape[0] % (16 * n) == 0
    )
    if not fits:
        return plain(hidden, grad_out, proj_in, proj_out, inv_out, inv_in, queries)
    steps = n // 4
    local_p = rank // n
    qrows = queries.shape[0] // n
    vmem = pl.BlockSpec(memory_space=pltpu.VMEM)
    hbm = pl.BlockSpec(memory_space=pl.ANY)
    return pl.pallas_call(
        functools.partial(kernel, n),
        out_shape=jax.ShapeDtypeStruct((qrows, n * seqs), F32),
        in_specs=[hbm, hbm, vmem, vmem, vmem, vmem, hbm],
        out_specs=vmem,
        scratch_shapes=[
            pltpu.VMEM(hidden.shape, BF16),
            pltpu.VMEM(grad_out.shape, BF16),
            pltpu.VMEM(queries.shape, BF16),
            pltpu.VMEM((tok, rank), F32),
            pltpu.VMEM((tok, rank), F32),
            pltpu.VMEM((rank, seqs, rank), F32),
            pltpu.VMEM((n, local_p * seqs, rank), BF16),
            pltpu.VMEM((n, local_p * seqs, rank), BF16),
            pltpu.VMEM((n * seqs, local_p * rank), BF16),
            *scatter_scratch(steps, tok, 2 * rank, F32),
            *scatter_scratch(steps, qrows, n * seqs, F32),
            pltpu.SemaphoreType.DMA((3, steps)),
            pltpu.SemaphoreType.DMA((3, 2, steps)),
            pltpu.SemaphoreType.DMA((3, 2, steps)),
            pltpu.SemaphoreType.DMA((2, n)),
        ],
        compiler_params=pltpu.CompilerParams(
            collective_id=0, has_side_effects=True, vmem_limit_bytes=58 * 1024 * 1024,
        ),
    )(hidden, grad_out, proj_in, proj_out, inv_out, inv_in, queries)


def solution(mesh):
    placed = (
        P("group", "feat"),
        P("group", "feat"),
        P("feat", None),
        P("feat", None),
        P(),
        P(),
        P(None, "feat"),
    )
    return jax.shard_map(
        on_device, mesh=mesh, in_specs=placed, out_specs=P("feat", "group"), check_vma=False
    )
```

time: 201 us -> 58 us (0.29)
  waiting for transfers between devices: 147 us -> 0 us
  Pallas kernels: 0 us -> 55.9 us
  matrix products: 21.2 us -> 0 us
  blocking collectives: 13.6 us -> 0 us
  between operations: 13.5 us -> 0.01 us
  other arithmetic: 3.32 us -> 0 us
    reduce_scatter x2 -> x0, waiting for transfers between devices: 147 us -> none  [the longest x1 75.5 us: on_device(): lax.psum_scatter(jnp.concatenate([in_part, out_part], axis=1), 'feat', sc...]
    pallas_call x0 -> x1, Pallas kernels: none -> 55.9 us  [on_device(): pl.pallas_call(functools.partial(kernel, n), out_shape=jax.ShapeDtypeStru...]
    dot_general x6 -> x0, matrix products: 21.2 us -> none  [the longest x1 13.2 us: on_device(): lax.dot_general(queries, tiles, contract, preferred_element_type=jnp.floa...]
    all_to_all x1 -> x0, blocking collectives: 13.6 us -> none  [on_device(): lax.all_to_all(conditioned, 'feat', split_axis=1, concat_axis=0, tiled=True)]
    concatenate x1 -> x0, other arithmetic: 2.35 us -> none  [on_device(): jnp.concatenate([in_part, out_part], axis=1)]
  transfers between devices with their start and end apart: 2 -> 0, of which waited for: 2 -> 0; matrix products, arithmetic and copies ran while one was open for 0% -> 0% of each run, Pallas kernels for 0% -> 0%
where the time goes in v1:
time: 58 us; the launch traced here: 57.6 us
  Pallas kernels  55.9 us (96%)
  local copies, waits for them, and re-layouts  1.67 us (3%)
    pallas_call x1, Pallas kernels, on_device(): pl.pallas_call(functools.partial(kernel, n), out_shape=jax.ShapeDtypeStru...  55.9 us
    unnamed x1, local copies, waits for them, and re-layouts  1.67 us

profile of v1, /device:TPU:0, one launch (start us, length us, event | category | flops | bytes accessed | tf_op | source)
XLA Modules:
  0.0 57.6 jit_solution(10471709516285001685)
XLA Ops:
  0.0 55.9 %shard_map.73 = f32[512,128]{1,0:T(8,128)} custom-call(bf16[4096,896]{1,0:T(8,128)(2,1)} %hid_hbm.1, bf16[4096,256]{1,0:T(8,128)(2,1)} %grad_hbm.1, bf16[896,128]{1,0:T(8,128)(2,1)} %pin_ref.1, bf16[256,128]{1,0:T(8,128)(2,1)} %pout_ref.1, f32[128,128]{1,0:T(8,128)} %iout_ref.1, f32[128,128]{1,0:T(8,128)} %iin_ref.1, bf16[8192,1024]{1,0:T(8,128)(2,1)} %que_hbm.1), custom_call_target="tpu_custom_call" | custom-call | tf_op jit(solution)/shard_map/pallas_call | solution.py:263
  55.9 1.7 %copy.9 = f32[512,128]{1,0:T(8,128)} copy(f32[512,128]{1,0:T(8,128)} %shard_map.73) | data formatting | bytes 524288

commit v2 on v1

v2 whole, which is shorter than its diff:
```python
import functools

import jax
import jax.numpy as jnp
from jax import lax
from jax.experimental import pallas as pl
from jax.experimental.pallas import tpu as pltpu
from jax.sharding import PartitionSpec as P

L = 32
LANES = 128
HALVES = 2
SCALE = 2.0 ** 48
F32 = jnp.float32
BF16 = jnp.bfloat16
EXACT = lax.Precision.HIGHEST


def plain(hidden, grad_out, proj_in, proj_out, inv_out, inv_in, queries):
    count_dev = lax.axis_size("feat")
    tok_rows = hidden.shape[0] // count_dev
    rank = proj_in.shape[1]
    in_part = jnp.dot(hidden, proj_in, preferred_element_type=F32)
    out_part = jnp.dot(grad_out, proj_out, preferred_element_type=F32)
    low_rows = lax.psum_scatter(
        jnp.concatenate([in_part, out_part], axis=1), "feat", scatter_dimension=0, tiled=True
    )
    in_low = low_rows[:, :rank].astype(BF16)
    out_low = low_rows[:, rank:].astype(BF16)
    seq_count = tok_rows // L
    in_seq = in_low.reshape(seq_count, L, rank)
    out_seq = out_low.reshape(seq_count, L, rank)
    per_example = jnp.einsum("elo,eli->eoi", out_seq, in_seq, preferred_element_type=F32)
    left = jnp.einsum("po,eoi->epi", inv_out, per_example, precision=EXACT)
    conditioned = jnp.einsum("epi,iq->epq", left, inv_in, precision=EXACT)
    conditioned = conditioned.reshape(seq_count, rank * rank).astype(BF16)
    contract = (((1,), (1,)), ((), ()))
    tiles = lax.all_to_all(conditioned, "feat", split_axis=1, concat_axis=0, tiled=True)
    return lax.psum_scatter(
        lax.dot_general(queries, tiles, contract, preferred_element_type=F32),
        "feat",
        scatter_dimension=0,
        tiled=True,
    )


def code_square(x):
    x = x * SCALE
    return (x * jnp.abs(x)).astype(BF16)


def decode_square(y):
    y = y.astype(F32)
    root = jnp.sqrt(jnp.abs(y)) * (1.0 / SCALE)
    return jnp.where(y < 0, -root, root)


def code_plain(x):
    return x.astype(BF16)


def decode_plain(y):
    return y.astype(F32)


class Scatter:
    def __init__(self, n, me, rows, bufs, sems, code, decode, product):
        self.steps = n // 4
        self.count = HALVES * self.steps
        self.c, self.b, self.a = me % 2, (me // 2) % 2, me // 4
        self.me, self.rows = me, rows
        self.own, self.csend, self.crecv, self.ysend, self.yrecv, self.zsend, self.zrecv = bufs
        self.sems = sems
        self.code, self.decode, self.product = code, decode, product

    def target(self, t):
        return (self.a + 1 + t) % self.steps

    def copy(self, stage, t, src, dst, to):
        return pltpu.make_async_remote_copy(
            src_ref=src, dst_ref=dst,
            send_sem=self.sems.at[stage, 0, t], recv_sem=self.sems.at[stage, 1, t],
            device_id={"feat": to}, device_id_type=pl.DeviceIdType.MESH,
        )

    def core(self, t, k):
        to = self.me + 1 - 2 * self.c
        return self.copy(k, t, self.csend.at[t, k], self.crecv.at[t, k], to)

    def side(self, t):
        return self.copy(2, t, self.ysend.at[t], self.yrecv.at[t], self.me + 2 - 4 * self.b)

    def far(self, t):
        to = self.target(t % self.steps) * 4 + self.me % 4
        return self.copy(3, t, self.zsend.at[t], self.zrecv.at[t], to)

    def term(self, t, k, c):
        b = self.b if k == 1 else 1 - self.b
        chunk = (self.target(t % self.steps) * 2 + b) * 2 + c
        return self.product(chunk * self.rows + (t // self.steps) * (self.rows // HALVES), self.rows // HALVES)

    def stage_core(self, t, entered):
        for k in range(2):
            self.csend[t, k] = self.term(t, k, 1 - self.c).astype(self.csend.dtype)
            if k == 0:
                entered()
            self.core(t, k).start()
        for k in range(2):
            self.own[t, k] = self.term(t, k, self.c)

    def stage_y(self, t):
        self.core(t, 0).wait_recv()
        self.ysend[t] = self.code(self.own[t, 0] + self.crecv[t, 0].astype(F32))
        self.side(t).start()

    def held(self, t):
        self.core(t, 1).wait_recv()
        self.side(t).wait_recv()
        return self.own[t, 1] + self.crecv[t, 1].astype(F32) + self.decode(self.yrecv[t])

    def stage_z(self, t):
        self.zsend[t] = self.code(self.held(t))
        self.far(t).start()

    def result(self, h):
        base = h * self.steps
        total = self.held(base + self.steps - 1)
        for t in range(base, base + self.steps - 1):
            self.far(t).wait_recv()
            total = total + self.decode(self.zrecv[t])
        return total

    def run(self, ready, entered, done):
        for i in range(self.count + 2):
            if i < self.count:
                if i < self.steps:
                    ready(i)
                self.stage_core(i, entered if i == 0 else lambda: None)
            if 0 <= i - 1 < self.count:
                self.stage_y(i - 1)
            z = i - 3
            if z >= 0 and z % self.steps != self.steps - 1:
                self.stage_z(z)
            if z >= 0 and z % self.steps == 0 and z >= self.steps:
                done(z // self.steps - 1, self.result(z // self.steps - 1))
        done(HALVES - 1, self.result(HALVES - 1))

    def finish(self):
        for t in range(self.count):
            self.core(t, 0).wait_send()
            self.core(t, 1).wait_send()
            self.side(t).wait_send()
            if t % self.steps != self.steps - 1:
                self.far(t).wait_send()


def kernel(n, hid_hbm, grad_hbm, pin_ref, pout_ref, iout_ref, iin_ref, que_hbm, out_ref,
           hid, grad, que, low_in, low_out, condf, cond, got, flat, ct,
           own1, cs1, cr1, ys1, yr1, zs1, zr1,
           own2, cs2, cr2, ys2, yr2, zs2, zr2,
           load_sems, sems1, sems2, a2a_sems):
    me = lax.axis_index("feat")
    steps = n // 4
    rank = pin_ref.shape[1]
    tok = hid.shape[0] // n
    seqs = tok // L
    qrows = que.shape[0] // n
    local_p = rank // n

    barrier = pltpu.get_barrier_semaphore()
    core, side = me + 1 - 2 * (me % 2), me + 2 - 4 * ((me // 2) % 2)
    partners = [core, side] + [(me + 4 * j) % n for j in range(1, steps)]
    for partner in partners:
        pl.semaphore_signal(barrier, inc=1, device_id={"feat": partner},
                            device_id_type=pl.DeviceIdType.MESH)

    def entered():
        pl.semaphore_wait(barrier, len(partners))

    def project(start, size):
        at = pl.ds(pl.multiple_of(start, size), size)
        return jnp.concatenate([
            jnp.dot(hid[at, :], pin_ref[...], preferred_element_type=F32),
            jnp.dot(grad[at, :], pout_ref[...], preferred_element_type=F32),
        ], axis=1)

    def score(start, size):
        at = pl.ds(pl.multiple_of(start, size), size)
        return lax.dot_general(que[at, :], ct[...], (((1,), (1,)), ((), ())), preferred_element_type=F32)

    first = Scatter(n, me, tok, (own1, cs1, cr1, ys1, yr1, zs1, zr1), sems1, code_square, decode_square, project)
    second = Scatter(n, me, qrows, (own2, cs2, cr2, ys2, yr2, zs2, zr2), sems2, code_plain, decode_plain, score)

    def load(hbm, vmem, which, t):
        size = hbm.shape[0] // steps
        at = pl.ds(pl.multiple_of(first.target(t) * size, size), size)
        return pltpu.make_async_copy(hbm.at[at, :], vmem.at[at, :], load_sems.at[which, t])

    for t in range(steps):
        load(hid_hbm, hid, 0, t).start()
        load(grad_hbm, grad, 1, t).start()

    def ready1(t):
        load(hid_hbm, hid, 0, t).wait()
        load(grad_hbm, grad, 1, t).wait()
        if t == steps - 1:
            for s in range(steps):
                load(que_hbm, que, 2, s).start()

    part = seqs // HALVES
    block = part * local_p

    def tile(h, j, slot):
        return pltpu.make_async_remote_copy(
            src_ref=cond.at[h, (me + j) % n], dst_ref=got.at[h, slot],
            send_sem=a2a_sems.at[h, 0, j], recv_sem=a2a_sems.at[h, 1, j],
            device_id={"feat": (me + j) % n}, device_id_type=pl.DeviceIdType.MESH,
        )

    def condition(h, low):
        low_in[...] = jnp.dot(low[:, :rank], iin_ref[...], precision=EXACT, preferred_element_type=F32)
        low_out[...] = lax.dot_general(low[:, rank:], iout_ref[...], (((1,), (1,)), ((), ())),
                                       precision=EXACT, preferred_element_type=F32)
        for e in range(part):
            at = pl.ds(e * L, L)
            one = lax.dot_general(low_out[at, :], low_in[at, :], (((0,), (0,)), ((), ())),
                                  precision=EXACT, preferred_element_type=F32)
            condf[:, e] = one.reshape(n, local_p, rank)
        cond[h] = condf[...].reshape(n, block, rank).astype(BF16)
        for j in range(1, n):
            tile(h, j, me).start()
        got[h, me] = cond[h, me]

    first.run(ready1, entered, condition)

    for h in range(HALVES):
        for j in range(1, n):
            tile(h, j, (me + n - j) % n).wait_recv()
        for s in range(n):
            flat[pl.ds((s * HALVES + h) * block, block), :] = got[h, s].astype(F32)
    for p in range(local_p):
        ct[:, p * rank:(p + 1) * rank] = flat[pl.ds(p, n * seqs, stride=local_p), :].astype(BF16)

    def ready2(t):
        load(que_hbm, que, 2, t).wait()

    def store(h, total):
        out_ref[pl.ds(h * (qrows // HALVES), qrows // HALVES), :] = total

    second.run(ready2, lambda: None, store)
    first.finish()
    second.finish()
    for h in range(HALVES):
        for j in range(1, n):
            tile(h, j, me).wait_send()


def scatter_scratch(steps, rows, cols, core_type):
    count, rows = HALVES * steps, rows // HALVES
    return [
        pltpu.VMEM((count, 2, rows, cols), F32),
        pltpu.VMEM((count, 2, rows, cols), core_type),
        pltpu.VMEM((count, 2, rows, cols), core_type),
        pltpu.VMEM((count, rows, cols), BF16),
        pltpu.VMEM((count, rows, cols), BF16),
        pltpu.VMEM((count, rows, cols), BF16),
        pltpu.VMEM((count, rows, cols), BF16),
    ]


def on_device(hidden, grad_out, proj_in, proj_out, inv_out, inv_in, queries):
    n = lax.axis_size("feat")
    tokens, rank = hidden.shape[0], proj_in.shape[1]
    tok = tokens // n
    seqs = tok // L
    fits = (
        n % 4 == 0 and n > 4 and rank == LANES and rank % n == 0 and tok % L == 0 and seqs % (8 * HALVES // 2) == 0 and (rank // n) % 8 == 0
        and hidden.shape[1] % LANES == 0 and grad_out.shape[1] % LANES == 0
        and queries.shape[0] % (16 * HALVES * n) == 0
    )
    if not fits:
        return plain(hidden, grad_out, proj_in, proj_out, inv_out, inv_in, queries)
    steps = n // 4
    local_p = rank // n
    qrows = queries.shape[0] // n
    vmem = pl.BlockSpec(memory_space=pltpu.VMEM)
    hbm = pl.BlockSpec(memory_space=pl.ANY)
    return pl.pallas_call(
        functools.partial(kernel, n),
        out_shape=jax.ShapeDtypeStruct((qrows, n * seqs), F32),
        in_specs=[hbm, hbm, vmem, vmem, vmem, vmem, hbm],
        out_specs=vmem,
        scratch_shapes=[
            pltpu.VMEM(hidden.shape, BF16),
            pltpu.VMEM(grad_out.shape, BF16),
            pltpu.VMEM(queries.shape, BF16),
            pltpu.VMEM((tok // HALVES, rank), F32),
            pltpu.VMEM((tok // HALVES, rank), F32),
            pltpu.VMEM((n, seqs // HALVES, local_p, rank), F32),
            pltpu.VMEM((HALVES, n, local_p * seqs // HALVES, rank), BF16),
            pltpu.VMEM((HALVES, n, local_p * seqs // HALVES, rank), BF16),
            pltpu.VMEM((n * seqs * local_p, rank), F32),
            pltpu.VMEM((n * seqs, local_p * rank), BF16),
            *scatter_scratch(steps, tok, 2 * rank, F32),
            *scatter_scratch(steps, qrows, n * seqs, F32),
            pltpu.SemaphoreType.DMA((3, steps)),
            pltpu.SemaphoreType.DMA((4, 2, HALVES * steps)),
            pltpu.SemaphoreType.DMA((4, 2, HALVES * steps)),
            pltpu.SemaphoreType.DMA((HALVES, 2, n)),
        ],
        compiler_params=pltpu.CompilerParams(
            collective_id=0, has_side_effects=True, vmem_limit_bytes=58 * 1024 * 1024,
        ),
    )(hidden, grad_out, proj_in, proj_out, inv_out, inv_in, queries)


def solution(mesh):
    placed = (
        P("group", "feat"),
        P("group", "feat"),
        P("feat", None),
        P("feat", None),
        P(),
        P(),
        P(None, "feat"),
    )
    return jax.shard_map(
        on_device, mesh=mesh, in_specs=placed, out_specs=P("feat", "group"), check_vma=False
    )
```

time: 58 us -> 57.6 us (level)
  no operation moved by 1% of the time
where the time goes in v2:
time: 57.6 us; the launch traced here: 57.4 us
  Pallas kernels  55.7 us (97%)
  local copies, waits for them, and re-layouts  1.67 us (3%)
    pallas_call x1, Pallas kernels, on_device(): pl.pallas_call(functools.partial(kernel, n), out_shape=jax.ShapeDtypeStru...  55.7 us
    unnamed x1, local copies, waits for them, and re-layouts  1.67 us

profile of v2, /device:TPU:0, one launch (start us, length us, event | category | flops | bytes accessed | tf_op | source)
XLA Modules:
  0.0 57.4 jit_solution(984016824419771285)
XLA Ops:
  0.0 55.7 %shard_map.73 = f32[512,128]{1,0:T(8,128)} custom-call(bf16[4096,896]{1,0:T(8,128)(2,1)} %hid_hbm.1, bf16[4096,256]{1,0:T(8,128)(2,1)} %grad_hbm.1, bf16[896,128]{1,0:T(8,128)(2,1)} %pin_ref.1, bf16[256,128]{1,0:T(8,128)(2,1)} %pout_ref.1, f32[128,128]{1,0:T(8,128)} %iout_ref.1, f32[128,128]{1,0:T(8,128)} %iin_ref.1, bf16[8192,1024]{1,0:T(8,128)(2,1)} %que_hbm.1), custom_call_target="tpu_custom_call" | custom-call | tf_op jit(solution)/shard_map/pallas_call | solution.py:288
  55.8 1.7 %copy.9 = f32[512,128]{1,0:T(8,128)} copy(f32[512,128]{1,0:T(8,128)} %shard_map.73) | data formatting | bytes 524288

commit v3 on v2

--- a/solution.py
+++ b/solution.py
@@ -186,7 +186,7 @@
 
     def score(start, size):
         at = pl.ds(pl.multiple_of(start, size), size)
-        return lax.dot_general(que[at, :], ct[...], (((1,), (1,)), ((), ())), preferred_element_type=F32)
+        return jnp.dot(que[at, :], ct[...], preferred_element_type=F32)
 
     first = Scatter(n, me, tok, (own1, cs1, cr1, ys1, yr1, zs1, zr1), sems1, code_square, decode_square, project)
     second = Scatter(n, me, qrows, (own2, cs2, cr2, ys2, yr2, zs2, zr2), sems2, code_plain, decode_plain, score)
@@ -239,7 +239,7 @@
         for s in range(n):
             flat[pl.ds((s * HALVES + h) * block, block), :] = got[h, s].astype(F32)
     for p in range(local_p):
-        ct[:, p * rank:(p + 1) * rank] = flat[pl.ds(p, n * seqs, stride=local_p), :].astype(BF16)
+        ct[pl.ds(p * rank, rank), :] = flat[pl.ds(p, n * seqs, stride=local_p), :].T.astype(BF16)
 
     def ready2(t):
         load(que_hbm, que, 2, t).wait()
@@ -300,7 +300,7 @@
             pltpu.VMEM((HALVES, n, local_p * seqs // HALVES, rank), BF16),
             pltpu.VMEM((HALVES, n, local_p * seqs // HALVES, rank), BF16),
             pltpu.VMEM((n * seqs * local_p, rank), F32),
-            pltpu.VMEM((n * seqs, local_p * rank), BF16),
+            pltpu.VMEM((local_p * rank, n * seqs), BF16),
             *scatter_scratch(steps, tok, 2 * rank, F32),
             *scatter_scratch(steps, qrows, n * seqs, F32),
             pltpu.SemaphoreType.DMA((3, steps)),

time: 57.6 us -> 57.1 us (level)
  no operation moved by 1% of the time
where the time goes in v3:
time: 57.1 us; the launch traced here: 57 us
  Pallas kernels  55.3 us (97%)
  local copies, waits for them, and re-layouts  1.67 us (3%)
    pallas_call x1, Pallas kernels, on_device(): pl.pallas_call(functools.partial(kernel, n), out_shape=jax.ShapeDtypeStru...  55.3 us
    unnamed x1, local copies, waits for them, and re-layouts  1.67 us

profile of v3, /device:TPU:0, one launch (start us, length us, event | category | flops | bytes accessed | tf_op | source)
XLA Modules:
  0.0 57.0 jit_solution(11407688316925786011)
XLA Ops:
  0.0 55.3 %shard_map.73 = f32[512,128]{1,0:T(8,128)} custom-call(bf16[4096,896]{1,0:T(8,128)(2,1)} %hid_hbm.1, bf16[4096,256]{1,0:T(8,128)(2,1)} %grad_hbm.1, bf16[896,128]{1,0:T(8,128)(2,1)} %pin_ref.1, bf16[256,128]{1,0:T(8,128)(2,1)} %pout_ref.1, f32[128,128]{1,0:T(8,128)} %iout_ref.1, f32[128,128]{1,0:T(8,128)} %iin_ref.1, bf16[8192,1024]{1,0:T(8,128)(2,1)} %que_hbm.1), custom_call_target="tpu_custom_call" | custom-call | tf_op jit(solution)/shard_map/pallas_call | solution.py:288
  55.3 1.7 %copy.9 = f32[512,128]{1,0:T(8,128)} copy(f32[512,128]{1,0:T(8,128)} %shard_map.73) | data formatting | bytes 524288
